TPU v7x, 32 devices: a whole 2x2x4 slice. The times are simulated.
32 devices in a mesh: parts: 2 (over y), fsdp: 4 (over z), tok: 4 (over x, core).
Axes of the slice: x: 2, y: 2, z: 4, core: 2. Of those that a mesh axis runs over, the one named last changes fastest.
Arguments:
- tokens: bfloat16 [64, 6144], P(('parts', 'fsdp', 'tok')), parts along dimension 0, may hold values from -6 to 6
- route_logits: bfloat16 [64, 2], P(('parts', 'fsdp', 'tok')), parts along dimension 0, may hold values from -6 to 6
- expert_ids: int32 [64, 2], P(('parts', 'fsdp', 'tok')), parts along dimension 0, may hold values from 0 to 7, all different within a row
- gate_weight: bfloat16 [6144, 16384], P('tok', 'fsdp'), may hold values from -0.078125 to 0.078125
- up_weight: bfloat16 [6144, 16384], P('tok', 'fsdp'), may hold values from -0.078125 to 0.078125
- down_weight: bfloat16 [16384, 6144], P(('fsdp', 'tok')), may hold values from -0.046875 to 0.046875
- a_factors: bfloat16 [8, 512, 6144], P(None, 'fsdp'), may hold values from -0.078125 to 0.078125
- b_factors: bfloat16 [8, 2, 256, 16384], P(None, None, 'tok', 'fsdp'), may hold values from -0.25 to 0.25
Outputs:
- mixed: bfloat16 [64, 6144], P(('parts', 'fsdp', 'tok')), parts along dimension 0
There are 2 independent parts, one for each index of `parts`. A program takes and returns all parts, laid end to end along the dimension named above; an argument that names none is the same for every part. Nothing has to cross between parts.
Inputs may be any that keep to these rules, and one draw needn't show every extreme that they name: `expert_ids`: every row names 2 different experts.
All inputs are finite; a program needn't handle non-finite values.
Results may differ from a plain program's by a relative error of at most 0.0055.
Values may be sent and summed in bfloat16 or wider, within the bound.
A program may use at most 512 MiB of HBM per device.

v0:
```python
import jax
import jax.numpy as jnp
from jax import lax
from jax.sharding import PartitionSpec as P

BOTH = ("fsdp", "tok")


def per_device(
    tokens, route_logits, expert_ids, gate_weight, up_weight, down_weight, a_factors, b_factors
):
    tok_size = lax.axis_size("tok")
    tok_at = lax.axis_index("tok")
    experts, own_ranks, _ = a_factors.shape
    depth, width = gate_weight.shape
    cut = b_factors.shape[2]
    rank = cut * tok_size
    share = experts // tok_size

    token_here = lax.all_gather(tokens, BOTH, axis=0, tiled=True)
    logit_here = lax.all_gather(route_logits, BOTH, axis=0, tiled=True)
    ident_here = lax.all_gather(expert_ids, BOTH, axis=0, tiled=True)
    count, topk = ident_here.shape

    a_here = lax.dynamic_slice_in_dim(a_factors, tok_at * share, share, axis=0)
    partial_codes = jnp.einsum(
        "rd,ejd->erj", token_here, a_here, preferred_element_type=jnp.float32
    ).astype(jnp.bfloat16)
    whole_codes = lax.all_gather(partial_codes, "tok", axis=0, tiled=True)
    whole_codes = lax.all_gather(whole_codes, "fsdp", axis=2, tiled=True)

    token_part = lax.dynamic_slice_in_dim(token_here, tok_at * depth, depth, axis=1)
    base_gate = jnp.dot(token_part, gate_weight, preferred_element_type=jnp.float32)
    base_up = jnp.dot(token_part, up_weight, preferred_element_type=jnp.float32)
    chosen = ident_here.T[:, :, None] == jnp.arange(experts, dtype=jnp.int32)

    def delta(which):
        codes = lax.dynamic_slice_in_dim(whole_codes, which * rank + tok_at * cut, cut, axis=2)
        spread = jnp.where(chosen[:, :, :, None], codes.transpose(1, 0, 2)[None], 0)
        return jnp.dot(
            spread.reshape(topk * count, experts * cut),
            b_factors[:, which].reshape(experts * cut, width),
            preferred_element_type=jnp.float32,
        ).reshape(topk, count, width)

    both = jnp.stack([base_gate + delta(0), base_up + delta(1)])
    both = lax.psum_scatter(both, "tok", scatter_dimension=3, tiled=True)
    scores = logit_here.astype(jnp.float32)
    first = jax.nn.sigmoid(scores[:, 0] - scores[:, 1])
    mixing = jnp.stack([first, 1.0 - first], axis=0)
    hidden = jnp.sum(mixing[:, :, None] * jax.nn.silu(both[0]) * both[1], axis=0)
    summed = jnp.dot(
        hidden.astype(jnp.bfloat16), down_weight, preferred_element_type=jnp.float32
    )
    return lax.psum_scatter(summed, BOTH, scatter_dimension=0, tiled=True).astype(jnp.bfloat16)


def solution(mesh):
    placed = (
        P(("parts", "fsdp", "tok"), None),
        P(("parts", "fsdp", "tok"), None),
        P(("parts", "fsdp", "tok"), None),
        P("tok", "fsdp"),
        P("tok", "fsdp"),
        P(("fsdp", "tok"), None),
        P(None, "fsdp", None),
        P(None, None, "tok", "fsdp"),
    )
    return jax.shard_map(
        per_device,
        mesh=mesh,
        in_specs=placed,
        out_specs=P(("parts", "fsdp", "tok"), None),
        check_vma=False,
    )
```

profile of v0, /device:TPU:0, one launch (start us, length us, event | category | flops | bytes accessed | tf_op | source)
XLA Modules:
  0.0 208.6 jit_solution(8187878687762231715)
XLA Ops:
  6.5 0.0 reduce-scatter.2.cloned.1.call-start
  6.5 24.4 %all-gather.1 = bf16[16,2,6144]{2,1,0:T(2,128)(2,1)S(1)} all-gather(bf16[1,2,6144]{2,1,0:T(2,128)(2,1)} %bitcast.53), channel_id=1, replica_groups=mesh['parts'=2,'fsdp'=4,'tok'=4] {'fsdp','tok'}, dimensions={0}, use_global_device_ids=true | all-gather | bytes 417792 | tf_op jit(solution)/shard_map/all_gather | solution.py:20
  30.9 0.1 reshape.112
  31.1 0.1 reshape.108
  31.2 2.9 %fusion.7 = bf16[2,32,128]{2,1,0:T(8,128)(2,1)S(1)} fusion(bf16[32,6144,1]{1,0,2:T(8,128)(2,1)S(1)} %reshape.112, bf16[8,128,6144]{2,1,0:T(8,128)(2,1)} %param.14, s32[]{:T(128)S(6)} %select_n.42), kind=kOutput, calls=%fused_computation.8 | convolution fusion | flops 100671488 | bytes 3555332 | tf_op jit(solution)/shard_map/rd,ejd->erj/dot_general | solution.py:26
  34.2 5.2 %all_gather.18 = bf16[8,32,128]{2,1,0:T(8,128)(2,1)S(1)} all-gather(bf16[2,32,128]{2,1,0:T(8,128)(2,1)S(1)} %fusion.7), channel_id=1, replica_groups=mesh['parts'=2,'fsdp'=4,'tok'=4] {'tok'}, dimensions={0}, use_global_device_ids=true | all-gather | bytes 81920 | tf_op jit(solution)/shard_map/all_gather | solution.py:29
  39.4 13.4 %all_gather.19 = bf16[8,32,512]{2,1,0:T(8,128)(2,1)S(1)} all-gather(bf16[8,32,128]{2,1,0:T(8,128)(2,1)S(1)} %all_gather.18), channel_id=1, replica_groups=mesh['parts'=2,'fsdp'=4,'tok'=4] {'fsdp'}, dimensions={2}, use_global_device_ids=true | all-gather | bytes 327680 | tf_op jit(solution)/shard_map/all_gather | solution.py:30
  52.9 0.1 dynamic-slice_bitcast_fusion.1
  53.0 17.7 %all-gather.2 = s32[16,2,2]{2,1,0:T(2,128)S(1)} all-gather(s32[1,2,2]{2,1,0:T(2,128)} %bitcast.55), channel_id=1, replica_groups=mesh['parts'=2,'fsdp'=4,'tok'=4] {'fsdp','tok'}, dimensions={0}, use_global_device_ids=true | all-gather | bytes 272 | tf_op jit(solution)/shard_map/all_gather | solution.py:22
  70.7 0.1 copy.26
  70.8 0.1 iota_compare_fusion
  70.9 0.1 broadcast_select_fusion.1
  71.0 0.1 select_n.45
  71.2 6.0 %fusion.21 = (bf16[8,1,64,4096]{3,2,1,0:T(8,128)(2,1)}, bf16[8,1,64,4096]{3,2,1,0:T(8,128)(2,1)}) fusion(bf16[8,2,64,4096]{3,2,1,0:T(8,128)(2,1)} %param.15), kind=kLoop, calls=%fused_computation.31 | loop fusion | bytes 16777216 | tf_op jit(solution)/shard_map/slice | solution.py:42
  77.1 0.1 select_n.48
  77.3 6.8 %fusion.14 = f32[32,4096]{1,0:T(8,128)S(1)} fusion(bf16[1536,4096]{1,0:T(8,128)(2,1)} %param.11, bf16[32,6144]{1,0:T(8,128)(2,1)S(1)} %reshape.108, s32[]{:T(128)S(6)} %select_n.41), kind=kOutput, calls=%fused_computation.17 | convolution fusion | flops 402653184 | bytes 13205508 | tf_op jit(solution)/shard_map/dot_general | solution.py:33
  84.1 0.0 copy-start.1
  84.1 0.0 copy-start
  84.1 7.0 %fusion.12 = f32[32,4096]{1,0:T(8,128)S(1)} fusion(bf16[1536,4096]{1,0:T(8,128)(2,1)} %param.12, bf16[32,6144]{1,0:T(8,128)(2,1)S(1)} %reshape.108, s32[]{:T(128)S(6)} %select_n.41), kind=kOutput, calls=%fused_computation.15 | convolution fusion | flops 402653184 | bytes 13205508 | tf_op jit(solution)/shard_map/dot_general | solution.py:34
  91.1 0.0 copy-done.1
  91.1 0.0 copy-start.2
  91.1 0.0 copy-start.3
  91.1 0.8 fusion.1
  92.0 0.0 copy-done
  92.0 0.8 fusion
  92.9 1.5 pad_maximum_fusion
  94.3 0.0 reduce-scatter.2.cloned.1.call-update
  94.4 0.0 copy-done.2
  94.4 18.7 %all-gather = bf16[16,2,2]{2,1,0:T(2,128)(2,1)S(1)} all-gather(bf16[1,2,2]{2,1,0:T(2,128)(2,1)S(1)} %bitcast.56), channel_id=1, replica_groups=mesh['parts'=2,'fsdp'=4,'tok'=4] {'fsdp','tok'}, dimensions={0}, use_global_device_ids=true | all-gather | bytes 136 | tf_op jit(solution)/shard_map/all_gather | solution.py:21
  113.0 0.1 copy.21
  113.1 0.1 copy.22
  113.2 0.1 reshape.111
  113.3 0.0 copy-done.3
  113.4 0.6 dynamic-slice
  114.6 9.7 %reduce-scatter.2.cloned.1.call-done = f32[2,2,32,1024]{3,2,1,0:T(8,128)} async-done(((f32[2,2,32,4096]{3,2,1,0:T(8,128)}), f32[2,2,32,1024]{3,2,1,0:T(8,128)}) %reduce-scatter.2.cloned.1.call-update) | async-done | bytes 524304 | tf_op jit(solution)/shard_map/reduce_scatter | solution.py:47
  124.3 1.1 fusion.11
  125.5 6.8 %fusion.22 = f32[32,6144]{1,0:T(8,128)S(1)} fusion(bf16[32,1024]{1,0:T(8,128)(2,1)S(1)} %fusion.11, bf16[1024,6144]{1,0:T(8,128)(2,1)} %param.13), kind=kOutput, calls=%fused_computation.32 | convolution fusion | flops 402653184 | bytes 13434880 | tf_op jit(solution)/shard_map/dot_general | solution.py:52
  132.3 68.7 %all-reduce.2 = bf16[32,6144]{1,0:T(8,128)(2,1)S(1)} all-reduce(f32[32,6144]{1,0:T(8,128)S(1)} %fusion.22), channel_id=3, replica_groups=mesh['parts'=2,'fsdp'=4,'tok'=4] {'fsdp','tok'}, use_global_device_ids=true, to_apply=%region_2.3.clone | all-reduce | flops 196608 | bytes 1179648
  201.1 0.6 dynamic-slice_convert_fusion
  (4 shorter events, 0.1 us)
Async XLA Ops:
  6.5 117.8 %reduce-scatter.2.cloned.1.call-start = ((), (), s32[]{:S(2)}) async-start(), calls=%async_computation.1 | async-start | bytes 2621440 | tf_op jit(solution)/shard_map/reduce_scatter | solution.py:47
  84.1 7.0 %copy-start.1 = (bf16[8,1,64,4096]{3,2,1,0:T(8,128)(2,1)S(1)}, bf16[8,1,64,4096]{3,2,1,0:T(8,128)(2,1)}, u32[]{:S(2)}) copy-start(bf16[8,1,64,4096]{3,2,1,0:T(8,128)(2,1)} %get-tuple-element.7) | copy-start | bytes 12582916
  84.1 7.9 %copy-start = (bf16[8,1,64,4096]{3,2,1,0:T(8,128)(2,1)S(1)}, bf16[8,1,64,4096]{3,2,1,0:T(8,128)(2,1)}, u32[]{:S(2)}) copy-start(bf16[8,1,64,4096]{3,2,1,0:T(8,128)(2,1)} %get-tuple-element.8) | copy-start | bytes 12582916
  91.1 3.3 %copy-start.2 = (bf16[2,2]{1,0:T(2,128)(2,1)S(1)}, bf16[2,2]{1,0:T(2,128)(2,1)}, u32[]{:S(2)}) copy-start(bf16[2,2]{1,0:T(2,128)(2,1)} %param.9) | copy-start | bytes 28
  91.1 22.2 %copy-start.3 = (u32[32]{0:T(128)S(1)}, u32[32]{0:T(128)}, u32[]{:S(2)}) copy-start(u32[32]{0:T(128)} %constant.35) | copy-start | bytes 388
Sparse Core Ops, SparseCore 0:
  94.5 29.8 reduce-scatter.1
where the time goes:
time: 209 us
  blocking collectives  148 us (71%)
  matrix products  25.3 us (12%)
  between operations  14.2 us (7%)
  waiting for transfers between devices  9.74 us (5%)
  local copies, waits for them, and re-layouts  8.33 us (4%)
  other arithmetic  2.85 us (1%)
    unnamed x1, blocking collectives  68.7 us
    all_gather x1, blocking collectives, per_device(): token_here = lax.all_gather(tokens, BOTH, axis=0, tiled=True)  24.4 us
    all_gather x1, blocking collectives, per_device(): logit_here = lax.all_gather(route_logits, BOTH, axis=0, tiled=True)  18.7 us
    all_gather x1, blocking collectives, per_device(): ident_here = lax.all_gather(expert_ids, BOTH, axis=0, tiled=True)  17.7 us
    all_gather x1, blocking collectives, per_device(): whole_codes = lax.all_gather(whole_codes, 'fsdp', axis=2, tiled=True)  13.4 us
    reduce_scatter x1, waiting for transfers between devices, per_device(): both = lax.psum_scatter(both, 'tok', scatter_dimension=3, tiled=True)  9.72 us
    dot_general x1, matrix products, per_device(): base_up = jnp.dot(token_part, up_weight, preferred_element_type=jnp.float32)  6.99 us
    dot_general x1, matrix products, per_device(): jnp.dot(token_part, gate_weight, preferred_element_type=jnp.float32)  6.84 us
  transfers between devices with their start and end apart: 1, of which 1 were waited for; matrix products, arithmetic and copies ran while one was open for 0% of the time, Pallas kernels for 0%

commit v1 on v0

--- a/solution.py
+++ b/solution.py
@@ -1,9 +1,340 @@
 import jax
 import jax.numpy as jnp
 from jax import lax
+from jax.experimental import pallas as pl
+from jax.experimental.pallas import tpu as pltpu
 from jax.sharding import PartitionSpec as P
 
 BOTH = ("fsdp", "tok")
+MESH = pl.DeviceIdType.MESH
+F32, BF16 = jnp.float32, jnp.bfloat16
+EXTRA = 128
+
+
+def one_hot_rows(rows, source_of):
+    row = lax.broadcasted_iota(jnp.int32, (rows, rows), 0)
+    column = lax.broadcasted_iota(jnp.int32, (rows, rows), 1)
+    return jnp.where(column == source_of(row), 1.0, 0.0).astype(BF16)
+
+
+def dot(left, right):
+    return jnp.dot(left, right, preferred_element_type=F32)
+
+
+def layer_kernel(
+    pack, wg_hbm, wu_hbm, wd_hbm, a_hbm, b_hbm, out,
+    wg, wu, wd, av, bv, held, y_all, y_own, extra, code_send, code_slot, spread,
+    base, far_sum, near_sum, near_send, far_send, x_send, near_got, far_got, x_got,
+    summed, down_got, row_send, row_got, z_send, z_got,
+    load_sem, tok_send_sem, tok_recv_sem, code_send_sem, code_recv_sem,
+    part_send_sem, part_recv_sem, down_send_sem, down_recv_sem,
+):
+    f, t = lax.axis_index("fsdp"), lax.axis_index("tok")
+    core_peer, x_peer, cross = (5 - t) % 4, (t + 2) % 4, 3 - t
+    x_at = t // 2
+    piece = pack.shape[1] - EXTRA
+    depth, chunk = wg.shape[1], wg.shape[2]
+    cut = b_hbm.shape[2]
+    count = y_own.shape[0]
+    order = (cross, x_peer, core_peer, t)
+
+    def columns(j):
+        return pl.ds(pl.multiple_of(order[j] * chunk, chunk), chunk)
+
+    def load(index, source, target):
+        return pltpu.make_async_copy(source, target, load_sem.at[index])
+
+    def remote(source, target, send, recv, to_f, to_t):
+        return pltpu.make_async_remote_copy(
+            src_ref=source, dst_ref=target, send_sem=send, recv_sem=recv,
+            device_id={"fsdp": to_f, "tok": to_t}, device_id_type=MESH,
+        )
+
+    a_loads = [
+        load(2 * h + e, a_hbm.at[2 * t + e, pl.ds(h * cut, cut)], av.at[h, e])
+        for h in range(2) for e in range(2)
+    ]
+    g_loads = [load(4 + j, wg_hbm.at[:, columns(j)], wg.at[j]) for j in range(4)]
+    u_loads = [load(8 + j, wu_hbm.at[:, columns(j)], wu.at[j]) for j in range(4)]
+    b_loads = [load(12 + j, b_hbm.at[:, :, :, columns(j)], bv.at[j]) for j in range(4)]
+    d_load = load(16, wd_hbm, wd)
+    for copy in a_loads + [g_loads[0], u_loads[0], g_loads[1], u_loads[1], b_loads[0], b_loads[1]]:
+        copy.start()
+
+    barrier = pltpu.get_barrier_semaphore()
+    me = f * 4 + t
+    for step in range(1, 16):
+        other = (me + step) % 16
+        pl.semaphore_signal(
+            barrier, inc=1, device_id={"fsdp": other // 4, "tok": other % 4}, device_id_type=MESH
+        )
+    pl.semaphore_wait(barrier, 15)
+
+    held[t, f] = pack[...]
+    sends = []
+    for step in range(1, 4):
+        copy = remote(
+            pack, held.at[t, f], tok_send_sem.at[step], tok_recv_sem.at[step], (f + step) % 4, t
+        )
+        copy.start()
+        sends.append(copy)
+    for copy in sends:
+        copy.wait_recv()
+    to_core = remote(held.at[t], held.at[t], tok_send_sem.at[4], tok_recv_sem.at[4], f, core_peer)
+    to_x = remote(held.at[t], held.at[t], tok_send_sem.at[5], tok_recv_sem.at[5], f, x_peer)
+    to_x.start()
+    to_core.start()
+    to_x.wait_recv()
+    onward = remote(
+        held.at[x_peer], held.at[x_peer], tok_send_sem.at[6], tok_recv_sem.at[6], f, core_peer
+    )
+    onward.start()
+    sends += [to_core, to_x, onward]
+    to_core.wait_recv()
+    onward.wait_recv()
+    for copy in [g_loads[2], u_loads[2], b_loads[2], g_loads[3], u_loads[3], b_loads[3], d_load]:
+        copy.start()
+
+    order_in = one_hot_rows(
+        8 * count, lambda r: ((r & 31) >> 1) * 16 + (r & 1) * 8 + (r >> 5)
+    )
+    turned = dot(order_in, held[...].reshape(8 * count, piece + EXTRA))
+    y_all[...] = turned[:, :piece].astype(BF16)
+    extra[...] = turned[:count, piece:]
+    for half in range(2):
+        rows = pl.ds(pl.multiple_of((2 * t + half) * count, count), count)
+        y_own[:, half * piece:(half + 1) * piece] = y_all[rows]
+
+    for copy in a_loads:
+        copy.wait()
+    ranks = 4 * cut
+    codes = jnp.zeros((count, ranks), F32)
+    for c in range(8):
+        codes += lax.dot_general(
+            y_all[c * count:(c + 1) * count],
+            av[:, :, :, c * piece:(c + 1) * piece].reshape(ranks, piece),
+            (((1,), (1,)), ((), ())),
+            preferred_element_type=F32,
+        )
+    for h in range(2):
+        code_send[h] = codes[:, h * 2 * cut:(h + 1) * 2 * cut].astype(BF16)
+    fx, fhalf = f % 2, f // 2
+    for step in range(4):
+        for h in range(2):
+            copy = remote(
+                code_send.at[h], code_slot.at[fhalf, t], code_send_sem.at[step * 2 + h],
+                code_recv_sem.at[fhalf * 4 + t], (f + step) % 4, 2 * fx + h,
+            )
+            if step == 0:
+                here = t == 2 * fx + h
+
+                @pl.when(here)
+                def _():
+                    code_slot[fhalf, t] = code_send[h]
+
+                @pl.when(jnp.logical_not(here))
+                def _():
+                    copy.start()
+            else:
+                copy.start()
+
+    def base_of(j):
+        g_loads[j].wait()
+        base[j, 0] = dot(y_own[...], wg[j])
+        u_loads[j].wait()
+        base[j, 1] = dot(y_own[...], wu[j])
+
+    base_of(0)
+    base_of(1)
+    for which in range(2):
+        for source in range(4):
+            mine = jnp.logical_and(fx == x_at, jnp.logical_and(fhalf == which, t == source))
+
+            @pl.when(jnp.logical_not(mine))
+            def _():
+                remote(
+                    code_send.at[0], code_slot.at[which, source], code_send_sem.at[0],
+                    code_recv_sem.at[which * 4 + source], f, x_peer,
+                ).wait_recv()
+
+    lane = lax.broadcasted_iota(jnp.int32, (count, 2 * cut), 1)
+    ids = [extra[:, k:k + 1] for k in range(2)]
+    for source in range(4):
+        label = jnp.where(lane < cut, 2.0 * source, 2.0 * source + 1.0)
+        for which in range(2):
+            value = code_slot[which, source].astype(F32)
+            for k in range(2):
+                spread[which, k * count:(k + 1) * count, source * 2 * cut:(source + 1) * 2 * cut] = (
+                    jnp.where(ids[k] == label, value, 0.0).astype(BF16)
+                )
+
+    def partial(j, which):
+        right = bv[j, :, which].reshape(8 * cut, chunk)
+        here = base[j, which]
+        return dot(spread[which], right) + jnp.concatenate([here, here], axis=0)
+
+    high = 2 * count
+    b_loads[0].wait()
+    for which in range(2):
+        far_send[which * high:(which + 1) * high] = partial(0, which).astype(BF16)
+    far_copy = remote(far_send, far_got, part_send_sem.at[0], part_recv_sem.at[0], f, core_peer)
+    far_copy.start()
+    b_loads[1].wait()
+    for which in range(2):
+        far_sum[which * high:(which + 1) * high] = partial(1, which)
+    far_copy.wait_recv()
+    x_send[...] = (far_sum[...] + far_got[...].astype(F32)).astype(BF16)
+    x_copy = remote(x_send, x_got, part_send_sem.at[1], part_recv_sem.at[1], f, x_peer)
+    x_copy.start()
+    base_of(2)
+    b_loads[2].wait()
+    for which in range(2):
+        near_send[which * high:(which + 1) * high] = partial(2, which).astype(BF16)
+    near_copy = remote(near_send, near_got, part_send_sem.at[2], part_recv_sem.at[2], f, core_peer)
+    near_copy.start()
+    base_of(3)
+    b_loads[3].wait()
+    for which in range(2):
+        near_sum[which * high:(which + 1) * high] = partial(3, which)
+    near_copy.wait_recv()
+    x_copy.wait_recv()
+    whole = near_sum[...] + near_got[...].astype(F32) + x_got[...].astype(F32)
+    first = jax.nn.sigmoid(extra[:, 2:3] - extra[:, 3:4])
+    gate0, gate1 = whole[:count], whole[count:high]
+    up0, up1 = whole[high:high + count], whole[high + count:]
+    hidden = (
+        first * (gate0 * jax.nn.sigmoid(gate0)) * up0
+        + (1.0 - first) * (gate1 * jax.nn.sigmoid(gate1)) * up1
+    ).astype(BF16)
+
+    d_load.wait()
+    for c in range(8):
+        block = dot(hidden, wd[:, c * piece:(c + 1) * piece])
+        summed[:, :, c * piece:(c + 1) * piece] = block.reshape(4, count // 4, piece)
+    down_far = remote(
+        summed.at[cross], down_got.at[0], down_send_sem.at[0], down_recv_sem.at[0], f, core_peer
+    )
+    down_near = remote(
+        summed.at[core_peer], down_got.at[1], down_send_sem.at[1], down_recv_sem.at[1], f, core_peer
+    )
+    down_far.start()
+    down_near.start()
+    down_far.wait_recv()
+    wide = 4 * piece
+    rows = count // 4
+    far_rows = summed[x_peer] + down_got[0]
+    row_send[...] = jnp.concatenate([far_rows[:, :wide], far_rows[:, wide:]], axis=0).astype(BF16)
+    row_copy = remote(row_send, row_got, down_send_sem.at[2], down_recv_sem.at[2], f, x_peer)
+    row_copy.start()
+    down_near.wait_recv()
+    near_rows = summed[t] + down_got[1]
+    row_copy.wait_recv()
+    arrived = row_got[...].astype(F32)
+    near_rows += jnp.concatenate([arrived[:rows], arrived[rows:]], axis=1)
+    stacked = jnp.concatenate(
+        [near_rows[:, c * piece:(c + 1) * piece] for c in range(8)], axis=0
+    ).astype(BF16)
+    order_out = one_hot_rows(8 * rows, lambda r: (r & 7) * 8 + (r >> 4) * 2 + ((r >> 3) & 1))
+    z_send[...] = dot(order_out, stacked).astype(BF16).reshape(z_send.shape)
+    z_copies = []
+    for step in range(1, 4):
+        to_f = (f + step) % 4
+        copy = remote(
+            z_send.at[to_f], z_got.at[step - 1], down_send_sem.at[2 + step],
+            down_recv_sem.at[2 + step], to_f, t,
+        )
+        copy.start()
+        z_copies.append(copy)
+    total = z_send[f].astype(F32)
+    for step, copy in enumerate(z_copies):
+        copy.wait_recv()
+        total += z_got[step].astype(F32)
+    out[...] = total.astype(BF16)
+
+    for copy in sends + [far_copy, x_copy, near_copy, down_far, down_near, row_copy] + z_copies:
+        copy.wait_send()
+    for step in range(4):
+        for h in range(2):
+            copy = remote(
+                code_send.at[h], code_slot.at[fhalf, t], code_send_sem.at[step * 2 + h],
+                code_recv_sem.at[fhalf * 4 + t], (f + step) % 4, 2 * fx + h,
+            )
+            if step == 0:
+
+                @pl.when(jnp.logical_not(t == 2 * fx + h))
+                def _():
+                    copy.wait_send()
+            else:
+                copy.wait_send()
+
+
+def fits(mesh):
+    return mesh.shape["fsdp"] == 4 and mesh.shape["tok"] == 4
+
+
+def fused_device(
+    tokens, route_logits, expert_ids, gate_weight, up_weight, down_weight, a_factors, b_factors
+):
+    own, width = tokens.shape
+    piece = width // 8
+    depth, hidden_width = gate_weight.shape
+    chunk = hidden_width // 4
+    cut = b_factors.shape[2]
+    count = 16 * own
+    rows = count // 4
+    notes = jnp.concatenate([expert_ids.astype(BF16), route_logits], axis=1)
+    notes = jnp.pad(notes, ((0, 0), (0, EXTRA - notes.shape[1])))
+    notes = jnp.broadcast_to(notes[:, None, :], (own, 8, EXTRA)).reshape(own * 8, EXTRA)
+    pack = jnp.concatenate([tokens.reshape(own * 8, piece), notes], axis=1)
+    vmem = pl.BlockSpec(memory_space=pltpu.VMEM)
+    hbm = pl.BlockSpec(memory_space=pl.ANY)
+    part = (4 * count, chunk)
+    sems = pltpu.SemaphoreType.DMA
+    out = pl.pallas_call(
+        layer_kernel,
+        out_shape=jax.ShapeDtypeStruct((own * 8, piece), BF16),
+        in_specs=[vmem, hbm, hbm, hbm, hbm, hbm],
+        out_specs=vmem,
+        scratch_shapes=[
+            pltpu.VMEM((4, depth, chunk), BF16),
+            pltpu.VMEM((4, depth, chunk), BF16),
+            pltpu.VMEM(down_weight.shape, BF16),
+            pltpu.VMEM((2, 2, cut, width), BF16),
+            pltpu.VMEM((4, 8, 2, cut, chunk), BF16),
+            pltpu.VMEM((4, 4, own * 8, piece + EXTRA), BF16),
+            pltpu.VMEM((8 * count, piece), BF16),
+            pltpu.VMEM((count, depth), BF16),
+            pltpu.VMEM((count, EXTRA), F32),
+            pltpu.VMEM((2, count, 2 * cut), BF16),
+            pltpu.VMEM((2, 4, count, 2 * cut), BF16),
+            pltpu.VMEM((2, 2 * count, 8 * cut), BF16),
+            pltpu.VMEM((4, 2, count, chunk), F32),
+            pltpu.VMEM(part, F32),
+            pltpu.VMEM(part, F32),
+            pltpu.VMEM(part, BF16),
+            pltpu.VMEM(part, BF16),
+            pltpu.VMEM(part, BF16),
+            pltpu.VMEM(part, BF16),
+            pltpu.VMEM(part, BF16),
+            pltpu.VMEM(part, BF16),
+            pltpu.VMEM((4, rows, width), F32),
+            pltpu.VMEM((2, rows, width), F32),
+            pltpu.VMEM((2 * rows, width // 2), BF16),
+            pltpu.VMEM((2 * rows, width // 2), BF16),
+            pltpu.VMEM((4, own * 8, piece), BF16),
+            pltpu.VMEM((3, own * 8, piece), BF16),
+            sems((17,)),
+            sems((7,)), sems((7,)), sems((8,)), sems((8,)),
+            sems((3,)), sems((3,)), sems((6,)), sems((6,)),
+        ],
+        compiler_params=pltpu.CompilerParams(
+            collective_id=0, has_side_effects=True, vmem_limit_bytes=60 * 2**20
+        ),
+        cost_estimate=pl.CostEstimate(
+            flops=2 * count * 28 * 2**20, bytes_accessed=49 * 2**20, transcendentals=0
+        ),
+    )(pack, gate_weight, up_weight, down_weight, a_factors, b_factors)
+    return out.reshape(own, width)
 
 
 def per_device(
@@ -67,7 +398,7 @@
         P(None, None, "tok", "fsdp"),
     )
     return jax.shard_map(
-        per_device,
+        fused_device if fits(mesh) else per_device,
         mesh=mesh,
         in_specs=placed,
         out_specs=P(("parts", "fsdp", "tok"), None),

time: 209 us -> 48.8 us (0.23)
  blocking collectives: 148 us -> 0 us
  Pallas kernels: 0 us -> 44.3 us
  matrix products: 25.3 us -> 0 us
  between operations: 14.2 us -> 0.01 us
  waiting for transfers between devices: 9.74 us -> 0 us
  local copies, waits for them, and re-layouts: 8.33 us -> 2.12 us
    all_gather x5 -> x0, blocking collectives: 79.4 us -> none  [the longest x1 24.4 us: per_device(): token_here = lax.all_gather(tokens, BOTH, axis=0, tiled=True)]
    unnamed x1 -> x0, blocking collectives: 68.7 us -> none
    pallas_call x0 -> x1, Pallas kernels: none -> 44.3 us  [fused_device(): pl.pallas_call(layer_kernel, out_shape=jax.ShapeDtypeStruct((own * 8, pie...]
    dot_general x6 -> x0, matrix products: 25.3 us -> none  [the longest x1 6.99 us: per_device(): base_up = jnp.dot(token_part, up_weight, preferred_element_type=jnp.float32)]
    reduce_scatter x1 -> x0, waiting for transfers between devices: 9.72 us -> none  [per_device(): both = lax.psum_scatter(both, 'tok', scatter_dimension=3, tiled=True)]
    slice x1 -> x0, local copies, waits for them, and re-layouts: 5.96 us -> none  [delta(): b_factors[:, which].reshape(experts * cut, width)]
    reshape x0 -> x3, local copies, waits for them, and re-layouts: none -> 2.12 us  [the longest x1 1.36 us: fused_device(): return out.reshape(own, width)]
  transfers between devices with their start and end apart: 1 -> 0, of which waited for: 1 -> 0; matrix products, arithmetic and copies ran while one was open for 0% -> 0% of each run, Pallas kernels for 0% -> 0%
where the time goes in v1:
time: 48.8 us; the launch traced here: 48.4 us
  Pallas kernels  44.3 us (91%)
  local copies, waits for them, and re-layouts  2.12 us (4%)
  other arithmetic  2.02 us (4%)
    pallas_call x1, Pallas kernels, fused_device(): pl.pallas_call(layer_kernel, out_shape=jax.ShapeDtypeStruct((own * 8, pie...  44.3 us
    reshape x1, local copies, waits for them, and re-layouts, fused_device(): return out.reshape(own, width)  1.36 us

profile of v1, /device:TPU:0, one launch (start us, length us, event | category | flops | bytes accessed | tf_op | source)
XLA Modules:
  0.0 48.4 jit_solution(454354469628684571)
XLA Ops:
  0.0 0.7 %convert_element_type.5 = bf16[2,2]{1,0:T(2,128)(2,1)S(1)} convert(s32[2,2]{1,0:T(2,128)} %param.10) | non-fusion elementwise | flops 4 | bytes 24 | tf_op jit(solution)/shard_map/convert_element_type | solution.py:285
  0.7 0.7 %fusion.2 = bf16[2,128]{1,0:T(2,128)(2,1)S(1)} fusion(bf16[2,2]{1,0:T(2,128)(2,1)} %param.9, bf16[2,2]{1,0:T(2,128)(2,1)S(1)} %convert_element_type.5), kind=kLoop, calls=%fused_computation.5 | loop fusion | flops 1792 | bytes 528 | tf_op jit(solution)/shard_map/concatenate | solution.py:285
  1.4 0.8 %reshape.10 = bf16[16,768]{1,0:T(8,128)(2,1)S(1)} reshape(bf16[2,6144]{1,0:T(2,128)(2,1)} %param.8) | data formatting | bytes 49152 | tf_op jit(solution)/shard_map/reshape | solution.py:288
  2.2 0.6 %pad_maximum_fusion.pack = bf16[16,896]{1,0:T(8,128)(2,1)} fusion(bf16[16,128]{1,0:T(8,128)(2,1)S(1)} %broadcast_bitcast_fusion, bf16[16,768]{1,0:T(8,128)(2,1)S(1)} %reshape.10), kind=kLoop, calls=%fused_computation | loop fusion | flops 57344 | bytes 57344 | tf_op jit(solution)/shard_map/concatenate | solution.py:288
  2.8 44.3 %shard_map.82 = bf16[16,768]{1,0:T(8,128)(2,1)} custom-call(bf16[16,896]{1,0:T(8,128)(2,1)} %pad_maximum_fusion.pack, bf16[1536,4096]{1,0:T(8,128)(2,1)} %wg_hbm.1, bf16[1536,4096]{1,0:T(8,128)(2,1)} %wu_hbm.1, bf16[1024,6144]{1,0:T(8,128)(2,1)} %wd_hbm.1, bf16[8,128,6144]{2,1,0:T(8,128)(2,1)} %a_hbm.1, bf16[8,2,64,4096]{3,2,1,0:T(8,128)(2,1)} %b_hbm.1), custom_call_target="tpu_custom_call" | custom-call | flops 1879048192 | bytes 51380224 | tf_op jit(solution)/shard_map/pallas_call | solution.py:293
  47.1 1.4 %reshape.12 = bf16[2,6144]{1,0:T(2,128)(2,1)} reshape(bf16[16,768]{1,0:T(8,128)(2,1)} %shard_map.82) | data formatting | bytes 49152 | tf_op jit(solution)/shard_map/reshape | solution.py:337
  (1 shorter events, 0.0 us)

commit v2 on v1

--- a/solution.py
+++ b/solution.py
@@ -22,8 +22,8 @@
 
 
 def layer_kernel(
-    pack, wg_hbm, wu_hbm, wd_hbm, a_hbm, b_hbm, out,
-    wg, wu, wd, av, bv, held, y_all, y_own, extra, code_send, code_slot, spread,
+    tokens, logits, ids_in, wg_hbm, wu_hbm, wd_hbm, a_hbm, b_hbm, out,
+    pack, wg, wu, wd, av, bv, held, y_all, y_own, extra, code_send, code_slot, spread,
     base, far_sum, near_sum, near_send, far_send, x_send, near_got, far_got, x_got,
     summed, down_got, row_send, row_got, z_send, z_got,
     load_sem, tok_send_sem, tok_recv_sem, code_send_sem, code_recv_sem,
@@ -62,15 +62,24 @@
         copy.start()
 
     barrier = pltpu.get_barrier_semaphore()
-    me = f * 4 + t
-    for step in range(1, 16):
-        other = (me + step) % 16
+    for to_f, to_t in [((f + 1) % 4, t), ((f + 2) % 4, t), ((f + 3) % 4, t), (f, core_peer), (f, x_peer)]:
         pl.semaphore_signal(
-            barrier, inc=1, device_id={"fsdp": other // 4, "tok": other % 4}, device_id_type=MESH
+            barrier, inc=1, device_id={"fsdp": to_f, "tok": to_t}, device_id_type=MESH
         )
-    pl.semaphore_wait(barrier, 15)
-
+    mine = tokens[...].astype(F32)
+    own = mine.shape[0]
+    pack[:, :piece] = jnp.concatenate(
+        [mine[:, c * piece:(c + 1) * piece] for c in range(8)], axis=0
+    ).astype(BF16)
+    lanes = lax.broadcasted_iota(jnp.int32, (own, EXTRA), 1)
+    notes = jnp.zeros((own, EXTRA), F32)
+    for k in range(2):
+        notes = jnp.where(lanes == k, ids_in[...].astype(F32)[:, k:k + 1], notes)
+        notes = jnp.where(lanes == 2 + k, logits[...].astype(F32)[:, k:k + 1], notes)
+    pack[:, piece:] = jnp.concatenate([notes, jnp.zeros((7 * own, EXTRA), F32)], axis=0).astype(BF16)
     held[t, f] = pack[...]
+    pl.semaphore_wait(barrier, 5)
+
     sends = []
     for step in range(1, 4):
         copy = remote(
@@ -96,7 +105,7 @@
         copy.start()
 
     order_in = one_hot_rows(
-        8 * count, lambda r: ((r & 31) >> 1) * 16 + (r & 1) * 8 + (r >> 5)
+        8 * count, lambda r: ((r & 31) >> 1) * 16 + (r >> 5) * 2 + (r & 1)
     )
     turned = dot(order_in, held[...].reshape(8 * count, piece + EXTRA))
     y_all[...] = turned[:, :piece].astype(BF16)
@@ -208,51 +217,71 @@
     ).astype(BF16)
 
     d_load.wait()
-    for c in range(8):
-        block = dot(hidden, wd[:, c * piece:(c + 1) * piece])
-        summed[:, :, c * piece:(c + 1) * piece] = block.reshape(4, count // 4, piece)
-    down_far = remote(
-        summed.at[cross], down_got.at[0], down_send_sem.at[0], down_recv_sem.at[0], f, core_peer
-    )
-    down_near = remote(
-        summed.at[core_peer], down_got.at[1], down_send_sem.at[1], down_recv_sem.at[1], f, core_peer
-    )
-    down_far.start()
-    down_near.start()
-    down_far.wait_recv()
-    wide = 4 * piece
-    rows = count // 4
-    far_rows = summed[x_peer] + down_got[0]
-    row_send[...] = jnp.concatenate([far_rows[:, :wide], far_rows[:, wide:]], axis=0).astype(BF16)
-    row_copy = remote(row_send, row_got, down_send_sem.at[2], down_recv_sem.at[2], f, x_peer)
-    row_copy.start()
-    down_near.wait_recv()
-    near_rows = summed[t] + down_got[1]
-    row_copy.wait_recv()
-    arrived = row_got[...].astype(F32)
-    near_rows += jnp.concatenate([arrived[:rows], arrived[rows:]], axis=1)
-    stacked = jnp.concatenate(
-        [near_rows[:, c * piece:(c + 1) * piece] for c in range(8)], axis=0
-    ).astype(BF16)
-    order_out = one_hot_rows(8 * rows, lambda r: (r & 7) * 8 + (r >> 4) * 2 + ((r >> 3) & 1))
-    z_send[...] = dot(order_out, stacked).astype(BF16).reshape(z_send.shape)
-    z_copies = []
-    for step in range(1, 4):
-        to_f = (f + step) % 4
+    rows, wide, small = count // 4, 4 * piece, piece // 2
+    to_core_copies = []
+    for half in range(2):
+        for c in range(4):
+            at = half * wide + c * piece
+            block = dot(hidden, wd[:, at:at + piece])
+            summed[half, :, :, c * piece:(c + 1) * piece] = block.reshape(4, rows, piece)
+        pair = []
+        for which, source in enumerate((cross, core_peer)):
+            index = 2 * half + which
+            copy = remote(
+                summed.at[half, source], down_got.at[half, which],
+                down_send_sem.at[index], down_recv_sem.at[index], f, core_peer,
+            )
+            copy.start()
+            pair.append(copy)
+        to_core_copies.append(pair)
+    row_copies = []
+    for half in range(2):
+        to_core_copies[half][0].wait_recv()
+        far_rows = summed[half, x_peer] + down_got[half, 0]
+        row_send[half] = jnp.concatenate(
+            [far_rows[:, :wide // 2], far_rows[:, wide // 2:]], axis=0
+        ).astype(BF16)
         copy = remote(
-            z_send.at[to_f], z_got.at[step - 1], down_send_sem.at[2 + step],
-            down_recv_sem.at[2 + step], to_f, t,
+            row_send.at[half], row_got.at[half],
+            down_send_sem.at[4 + half], down_recv_sem.at[4 + half], f, x_peer,
         )
         copy.start()
-        z_copies.append(copy)
-    total = z_send[f].astype(F32)
-    for step, copy in enumerate(z_copies):
-        copy.wait_recv()
-        total += z_got[step].astype(F32)
-    out[...] = total.astype(BF16)
-
-    for copy in sends + [far_copy, x_copy, near_copy, down_far, down_near, row_copy] + z_copies:
+        row_copies.append(copy)
+    order_out = one_hot_rows(8 * rows, lambda r: ((r >> 1) & 7) * 8 + (r >> 4) * 2 + (r & 1))
+    z_copies = []
+    for half in range(2):
+        to_core_copies[half][1].wait_recv()
+        near_rows = summed[half, t] + down_got[half, 1]
+        row_copies[half].wait_recv()
+        arrived = row_got[half].astype(F32)
+        near_rows += jnp.concatenate([arrived[:rows], arrived[rows:]], axis=1)
+        stacked = jnp.concatenate(
+            [near_rows[:, c * small:(c + 1) * small] for c in range(8)], axis=0
+        ).astype(BF16)
+        z_send[half] = dot(order_out, stacked).astype(BF16).reshape(4, 2 * rows, small)
+        for step in range(1, 4):
+            to_f = (f + step) % 4
+            index = 5 + 3 * half + step
+            copy = remote(
+                z_send.at[half, to_f], z_got.at[half, step - 1],
+                down_send_sem.at[index], down_recv_sem.at[index], to_f, t,
+            )
+            copy.start()
+            z_copies.append(copy)
+    for half in range(2):
+        total = z_send[half, f].astype(F32)
+        for step in range(3):
+            z_copies[3 * half + step].wait_recv()
+            total += z_got[half, step].astype(F32)
+        out[:, half * wide:(half + 1) * wide] = jnp.concatenate(
+            [total[own * c:own * (c + 1)] for c in range(8)], axis=1
+        ).astype(BF16)
+
+    for copy in sends + [far_copy, x_copy, near_copy] + row_copies + z_copies:
         copy.wait_send()
+    for pair in to_core_copies:
+        for copy in pair:
+            copy.wait_send()
     for step in range(4):
         for h in range(2):
             copy = remote(
@@ -282,20 +311,17 @@
     cut = b_factors.shape[2]
     count = 16 * own
     rows = count // 4
-    notes = jnp.concatenate([expert_ids.astype(BF16), route_logits], axis=1)
-    notes = jnp.pad(notes, ((0, 0), (0, EXTRA - notes.shape[1])))
-    notes = jnp.broadcast_to(notes[:, None, :], (own, 8, EXTRA)).reshape(own * 8, EXTRA)
-    pack = jnp.concatenate([tokens.reshape(own * 8, piece), notes], axis=1)
     vmem = pl.BlockSpec(memory_space=pltpu.VMEM)
     hbm = pl.BlockSpec(memory_space=pl.ANY)
     part = (4 * count, chunk)
     sems = pltpu.SemaphoreType.DMA
     out = pl.pallas_call(
         layer_kernel,
-        out_shape=jax.ShapeDtypeStruct((own * 8, piece), BF16),
-        in_specs=[vmem, hbm, hbm, hbm, hbm, hbm],
+        out_shape=jax.ShapeDtypeStruct((own, width), BF16),
+        in_specs=[vmem, vmem, vmem, hbm, hbm, hbm, hbm, hbm],
         out_specs=vmem,
         scratch_shapes=[
+            pltpu.VMEM((own * 8, piece + EXTRA), BF16),
             pltpu.VMEM((4, depth, chunk), BF16),
             pltpu.VMEM((4, depth, chunk), BF16),
             pltpu.VMEM(down_weight.shape, BF16),
@@ -317,15 +343,15 @@
             pltpu.VMEM(part, BF16),
             pltpu.VMEM(part, BF16),
             pltpu.VMEM(part, BF16),
-            pltpu.VMEM((4, rows, width), F32),
-            pltpu.VMEM((2, rows, width), F32),
-            pltpu.VMEM((2 * rows, width // 2), BF16),
-            pltpu.VMEM((2 * rows, width // 2), BF16),
-            pltpu.VMEM((4, own * 8, piece), BF16),
-            pltpu.VMEM((3, own * 8, piece), BF16),
+            pltpu.VMEM((2, 4, rows, width // 2), F32),
+            pltpu.VMEM((2, 2, rows, width // 2), F32),
+            pltpu.VMEM((2, 2 * rows, width // 4), BF16),
+            pltpu.VMEM((2, 2 * rows, width // 4), BF16),
+            pltpu.VMEM((2, 4, own * 8, piece // 2), BF16),
+            pltpu.VMEM((2, 3, own * 8, piece // 2), BF16),
             sems((17,)),
             sems((7,)), sems((7,)), sems((8,)), sems((8,)),
-            sems((3,)), sems((3,)), sems((6,)), sems((6,)),
+            sems((3,)), sems((3,)), sems((12,)), sems((12,)),
         ],
         compiler_params=pltpu.CompilerParams(
             collective_id=0, has_side_effects=True, vmem_limit_bytes=60 * 2**20
@@ -333,8 +359,11 @@
         cost_estimate=pl.CostEstimate(
             flops=2 * count * 28 * 2**20, bytes_accessed=49 * 2**20, transcendentals=0
         ),
-    )(pack, gate_weight, up_weight, down_weight, a_factors, b_factors)
-    return out.reshape(own, width)
+    )(
+        tokens, route_logits, expert_ids,
+        gate_weight, up_weight, down_weight, a_factors, b_factors,
+    )
+    return out
 
 
 def per_device(

time: 48.8 us -> 43 us (0.88)
  Pallas kernels: 44.3 us -> 41.4 us
  other arithmetic: 2.02 us -> 0 us
  local copies, waits for them, and re-layouts: 2.12 us -> 1.36 us
    pallas_call x1, Pallas kernels: 44.3 us -> 41.4 us  [fused_device(): pl.pallas_call(layer_kernel, out_shape=jax.ShapeDtypeStruct((own, width),...]
    reshape x3 -> x0, local copies, waits for them, and re-layouts: 2.12 us -> none  [the longest x1 1.36 us: fused_device(): return out.reshape(own, width)]
    unnamed x0 -> x1, local copies, waits for them, and re-layouts: none -> 1.36 us
    concatenate x2 -> x0, other arithmetic: 1.33 us -> none  [the longest x1 0.73 us: fused_device(): notes = jnp.concatenate([expert_ids.astype(BF16), route_logits], axis=1)]
    convert_element_type x1 -> x0, other arithmetic: 0.68 us -> none  [fused_device(): notes = jnp.concatenate([expert_ids.astype(BF16), route_logits], axis=1)]
where the time goes in v2:
time: 43 us; the launch traced here: 42.8 us
  Pallas kernels  41.4 us (96%)
  local copies, waits for them, and re-layouts  1.36 us (3%)
    pallas_call x1, Pallas kernels, fused_device(): pl.pallas_call(layer_kernel, out_shape=jax.ShapeDtypeStruct((own, width),...  41.4 us
    unnamed x1, local copies, waits for them, and re-layouts  1.36 us

profile of v2, /device:TPU:0, one launch (start us, length us, event | category | flops | bytes accessed | tf_op | source)
XLA Modules:
  0.0 42.8 jit_solution(16792963805191448254)
XLA Ops:
  0.0 41.4 %shard_map.82 = bf16[2,6144]{1,0:T(2,128)(2,1)} custom-call(bf16[2,6144]{1,0:T(2,128)(2,1)} %tokens.1, bf16[2,2]{1,0:T(2,128)(2,1)} %logits.1, s32[2,2]{1,0:T(2,128)} %ids_in.1, bf16[1536,4096]{1,0:T(8,128)(2,1)} %wg_hbm.1, bf16[1536,4096]{1,0:T(8,128)(2,1)} %wu_hbm.1, bf16[1024,6144]{1,0:T(8,128)(2,1)} %wd_hbm.1, bf16[8,128,6144]{2,1,0:T(8,128)(2,1)} %a_hbm.1, ...), custom_call_target="tpu_custom_call" | custom-call | flops 1879048192 | bytes 51380224 | tf_op jit(solution)/shard_map/pallas_call | solution.py:318
  41.4 1.4 %copy.10 = bf16[2,6144]{1,0:T(2,128)(2,1)} copy(bf16[2,6144]{1,0:T(2,128)(2,1)} %shard_map.82) | data formatting | bytes 49152

commit v3 on v2

--- a/solution.py
+++ b/solution.py
@@ -24,7 +24,7 @@
 def layer_kernel(
     tokens, logits, ids_in, wg_hbm, wu_hbm, wd_hbm, a_hbm, b_hbm, out,
     pack, wg, wu, wd, av, bv, held, y_all, y_own, extra, code_send, code_slot, spread,
-    base, far_sum, near_sum, near_send, far_send, x_send, near_got, far_got, x_got,
+    base, near_sum, near_send, far_send, x_send, near_got, far_got, x_got,
     summed, down_got, row_send, row_got, z_send, z_got,
     load_sem, tok_send_sem, tok_recv_sem, code_send_sem, code_recv_sem,
     part_send_sem, part_recv_sem, down_send_sem, down_recv_sem,
@@ -87,20 +87,32 @@
         )
         copy.start()
         sends.append(copy)
-    for copy in sends:
+    along_x, along_core, onward = [], [], []
+    for step in (0, 1, 3, 2):
+        if step:
+            sends[step - 1].wait_recv()
+        block = held.at[t, (f + 4 - step) % 4]
+        to_x = remote(
+            block, block, tok_send_sem.at[4 + step], tok_recv_sem.at[4 + step], f, x_peer
+        )
+        to_core = remote(
+            block, block, tok_send_sem.at[8 + step], tok_recv_sem.at[8 + step], f, core_peer
+        )
+        to_x.start()
+        to_core.start()
+        along_x.append(to_x)
+        along_core.append(to_core)
+    for place, step in enumerate((0, 1, 3, 2)):
+        along_x[place].wait_recv()
+        block = held.at[x_peer, (f + 4 - step) % 4]
+        copy = remote(
+            block, block, tok_send_sem.at[12 + step], tok_recv_sem.at[12 + step], f, core_peer
+        )
+        copy.start()
+        onward.append(copy)
+    for copy in along_core + onward:
         copy.wait_recv()
-    to_core = remote(held.at[t], held.at[t], tok_send_sem.at[4], tok_recv_sem.at[4], f, core_peer)
-    to_x = remote(held.at[t], held.at[t], tok_send_sem.at[5], tok_recv_sem.at[5], f, x_peer)
-    to_x.start()
-    to_core.start()
-    to_x.wait_recv()
-    onward = remote(
-        held.at[x_peer], held.at[x_peer], tok_send_sem.at[6], tok_recv_sem.at[6], f, core_peer
-    )
-    onward.start()
-    sends += [to_core, to_x, onward]
-    to_core.wait_recv()
-    onward.wait_recv()
+    sends += along_x + along_core + onward
     for copy in [g_loads[2], u_loads[2], b_loads[2], g_loads[3], u_loads[3], b_loads[3], d_load]:
         copy.start()
 
@@ -183,30 +195,42 @@
         return dot(spread[which], right) + jnp.concatenate([here, here], axis=0)
 
     high = 2 * count
+    part_copies = []
+
+    def part_copy(source, target, kind, which, to_t):
+        at = pl.ds(which * high, high)
+        index = 2 * kind + which
+        copy = remote(
+            source.at[at], target.at[at], part_send_sem.at[index], part_recv_sem.at[index], f, to_t
+        )
+        copy.start()
+        part_copies.append(copy)
+        return copy
+
     b_loads[0].wait()
+    b_loads[1].wait()
+    far_copies, x_copies, near_copies = [], [], []
     for which in range(2):
-        far_send[which * high:(which + 1) * high] = partial(0, which).astype(BF16)
-    far_copy = remote(far_send, far_got, part_send_sem.at[0], part_recv_sem.at[0], f, core_peer)
-    far_copy.start()
-    b_loads[1].wait()
+        at = slice(which * high, (which + 1) * high)
+        far_send[at] = partial(0, which).astype(BF16)
+        far_copies.append(part_copy(far_send, far_got, 0, which, core_peer))
     for which in range(2):
-        far_sum[which * high:(which + 1) * high] = partial(1, which)
-    far_copy.wait_recv()
-    x_send[...] = (far_sum[...] + far_got[...].astype(F32)).astype(BF16)
-    x_copy = remote(x_send, x_got, part_send_sem.at[1], part_recv_sem.at[1], f, x_peer)
-    x_copy.start()
+        at = slice(which * high, (which + 1) * high)
+        own_sum = partial(1, which)
+        far_copies[which].wait_recv()
+        x_send[at] = (own_sum + far_got[at].astype(F32)).astype(BF16)
+        x_copies.append(part_copy(x_send, x_got, 1, which, x_peer))
     base_of(2)
     b_loads[2].wait()
     for which in range(2):
         near_send[which * high:(which + 1) * high] = partial(2, which).astype(BF16)
-    near_copy = remote(near_send, near_got, part_send_sem.at[2], part_recv_sem.at[2], f, core_peer)
-    near_copy.start()
+        near_copies.append(part_copy(near_send, near_got, 2, which, core_peer))
     base_of(3)
     b_loads[3].wait()
     for which in range(2):
         near_sum[which * high:(which + 1) * high] = partial(3, which)
-    near_copy.wait_recv()
-    x_copy.wait_recv()
+    for copy in near_copies + x_copies:
+        copy.wait_recv()
     whole = near_sum[...] + near_got[...].astype(F32) + x_got[...].astype(F32)
     first = jax.nn.sigmoid(extra[:, 2:3] - extra[:, 3:4])
     gate0, gate1 = whole[:count], whole[count:high]
@@ -277,7 +301,7 @@
             [total[own * c:own * (c + 1)] for c in range(8)], axis=1
         ).astype(BF16)
 
-    for copy in sends + [far_copy, x_copy, near_copy] + row_copies + z_copies:
+    for copy in sends + part_copies + row_copies + z_copies:
         copy.wait_send()
     for pair in to_core_copies:
         for copy in pair:
@@ -336,7 +360,6 @@
             pltpu.VMEM((2, 2 * count, 8 * cut), BF16),
             pltpu.VMEM((4, 2, count, chunk), F32),
             pltpu.VMEM(part, F32),
-            pltpu.VMEM(part, F32),
             pltpu.VMEM(part, BF16),
             pltpu.VMEM(part, BF16),
             pltpu.VMEM(part, BF16),
@@ -350,8 +373,8 @@
             pltpu.VMEM((2, 4, own * 8, piece // 2), BF16),
             pltpu.VMEM((2, 3, own * 8, piece // 2), BF16),
             sems((17,)),
-            sems((7,)), sems((7,)), sems((8,)), sems((8,)),
-            sems((3,)), sems((3,)), sems((12,)), sems((12,)),
+            sems((16,)), sems((16,)), sems((8,)), sems((8,)),
+            sems((6,)), sems((6,)), sems((12,)), sems((12,)),
         ],
         compiler_params=pltpu.CompilerParams(
             collective_id=0, has_side_effects=True, vmem_limit_bytes=60 * 2**20

time: 43 us -> 42.5 us (0.988)
  Pallas kernels: 41.4 us -> 40.9 us
    pallas_call x1, Pallas kernels: 41.4 us -> 40.9 us  [fused_device(): pl.pallas_call(layer_kernel, out_shape=jax.ShapeDtypeStruct((own, width),...]
where the time goes in v3:
time: 42.5 us; the launch traced here: 42.3 us
  Pallas kernels  40.9 us (96%)
  local copies, waits for them, and re-layouts  1.36 us (3%)
    pallas_call x1, Pallas kernels, fused_device(): pl.pallas_call(layer_kernel, out_shape=jax.ShapeDtypeStruct((own, width),...  40.9 us
    unnamed x1, local copies, waits for them, and re-layouts  1.36 us

profile of v3, /device:TPU:0, one launch (start us, length us, event | category | flops | bytes accessed | tf_op | source)
XLA Modules:
  0.0 42.3 jit_solution(16960304892986533249)
XLA Ops:
  0.0 40.9 %shard_map.82 = bf16[2,6144]{1,0:T(2,128)(2,1)} custom-call(bf16[2,6144]{1,0:T(2,128)(2,1)} %tokens.1, bf16[2,2]{1,0:T(2,128)(2,1)} %logits.1, s32[2,2]{1,0:T(2,128)} %ids_in.1, bf16[1536,4096]{1,0:T(8,128)(2,1)} %wg_hbm.1, bf16[1536,4096]{1,0:T(8,128)(2,1)} %wu_hbm.1, bf16[1024,6144]{1,0:T(8,128)(2,1)} %wd_hbm.1, bf16[8,128,6144]{2,1,0:T(8,128)(2,1)} %a_hbm.1, ...), custom_call_target="tpu_custom_call" | custom-call | flops 1879048192 | bytes 51380224 | tf_op jit(solution)/shard_map/pallas_call | solution.py:342
  40.9 1.4 %copy.10 = bf16[2,6144]{1,0:T(2,128)(2,1)} copy(bf16[2,6144]{1,0:T(2,128)(2,1)} %shard_map.82) | data formatting | bytes 49152
